TPU v7x, 32 devices: a whole 2x2x4 slice. The times are simulated.
32 devices in a mesh: replica: 4 (over y, x), rollout: 8 (over z, core).
Axes of the slice: x: 2, y: 2, z: 4, core: 2. Of those that a mesh axis runs over, the one named last changes fastest.
Arguments:
- w_query: bfloat16 [8192, 8192], P('replica', 'rollout'), may hold values from -6 to 6
- gate_weight: bfloat16 [8192, 28672], P('replica', 'rollout'), may hold values from -6 to 6
- w_output: bfloat16 [8192, 8192], P('rollout', 'replica'), may hold values from -6 to 6
- input_state: float32 [3, 3, 8192, 64], P(None, None, 'rollout', 'replica'), may hold values from -3 to 3, as said below
- input_parts: float32 [4, 3, 8192, 64], P('replica', None, 'rollout'), may hold values from -6 to 6
- square_state: float32 [2, 3, 64, 8192], P(None, None, 'replica', 'rollout'), may hold values from -3 to 3, as said below
- square_parts: float32 [4, 2, 64, 8192], P('replica', None, None, 'rollout'), may hold values from -6 to 6
- gate_state: float32 [3, 64, 28672], P(None, 'replica', 'rollout'), may hold values from -3 to 3, as said below
- gate_parts: float32 [4, 64, 28672], P('replica', None, 'rollout'), may hold values from -6 to 6
Outputs:
- merged_query: bfloat16 [8192, 8192], P('replica', 'rollout')
- merged_gate: bfloat16 [8192, 28672], P('replica', 'rollout')
- merged_output: bfloat16 [8192, 8192], P('rollout', 'replica')
- new_input_state: float32 [3, 3, 8192, 64], P(None, None, 'rollout', 'replica')
- new_square_state: float32 [2, 3, 64, 8192], P(None, None, 'replica', 'rollout')
- new_gate_state: float32 [3, 64, 28672], P(None, 'replica', 'rollout')
Inputs may be any that keep to these rules, and one draw needn't show every extreme that they name: `input_state`: along the dimension of size 3 the entries are the factor, its first moment and its second moment, the last one positive. `square_state`: along the dimension of size 3 the entries are the factor, its first moment and its second moment, the last one positive. `gate_state`: along the first dimension the entries are the factor, its first moment and its second moment, the last one positive.
All inputs are finite; a program needn't handle non-finite values.
Results may differ from a plain program's by a relative error of at most 0.0051.
Values may be sent and summed in bfloat16 or wider, within the bound.
A program may use at most 128 MiB of HBM per device.

v0:
```python
import jax
import jax.numpy as jnp
from jax import lax
from jax.sharding import PartitionSpec as P

STEP = 3


first_moment_decay = 0.9
beta_second = 0.999
learn_rate = 0.05
epsilon = 1e-08
adapter_scale = 2.0


def adam_update(param, first, second, grad):
    first_new = first_moment_decay * first + (1.0 - first_moment_decay) * grad
    second_new = beta_second * second + (1.0 - beta_second) * grad * grad
    fix_first = 1.0 - first_moment_decay**STEP
    fix_second = 1.0 - beta_second**STEP
    param_new = param - learn_rate * (first_new / fix_first) / (
        jnp.sqrt(second_new / fix_second) + epsilon
    )
    return (param_new, first_new, second_new)


def merge_weight(weight_matrix, left, right):
    weight_change = jnp.dot(left, right, preferred_element_type=jnp.float32)
    return (weight_matrix.astype(jnp.float32) + adapter_scale * weight_change).astype(jnp.bfloat16)


def on_device(
    w_query,
    gate_weight,
    w_output,
    input_state,
    input_parts,
    square_state,
    square_parts,
    gate_state,
    gate_parts,
):
    input_grad, square_grad, gate_gradient = (
        lax.psum_scatter(input_parts, "replica", scatter_dimension=3, tiled=True),
        lax.psum_scatter(square_parts, "replica", scatter_dimension=2, tiled=True),
        lax.psum_scatter(gate_parts, "replica", scatter_dimension=1, tiled=True),
    )
    new_input = jnp.stack(
        adam_update(input_state[:, 0], input_state[:, 1], input_state[:, 2], input_grad[0]), axis=1
    )
    new_square = jnp.stack(
        adam_update(square_state[:, 0], square_state[:, 1], square_state[:, 2], square_grad[0]),
        axis=1,
    )
    updated_gate_weight = jnp.stack(
        adam_update(gate_state[0], gate_state[1], gate_state[2], gate_gradient[0]), axis=0
    )
    input_factor = new_input[:, 0].astype(jnp.bfloat16)
    square_factor = new_square[:, 0].astype(jnp.bfloat16)
    gate_factor = updated_gate_weight[0].astype(jnp.bfloat16)
    column_slab, output_slab = (
        lax.all_gather(input_factor[:2], "rollout", axis=1, tiled=True),
        lax.all_gather(square_factor[1], "rollout", axis=1, tiled=True),
    )
    output_rows, query_columns, gate_column_span = (
        lax.all_gather(input_factor[2], "replica", axis=1, tiled=True),
        lax.all_gather(square_factor[0], "replica", axis=0, tiled=True),
        lax.all_gather(gate_factor, "replica", axis=0, tiled=True),
    )
    column_factor = lax.all_to_all(column_slab, "replica", split_axis=1, concat_axis=2, tiled=True)
    output_columns = lax.all_to_all(output_slab, "replica", split_axis=1, concat_axis=0, tiled=True)
    merged_query = merge_weight(w_query, column_factor[0], query_columns)
    merged_gate = merge_weight(gate_weight, column_factor[1], gate_column_span)
    merged_output = merge_weight(w_output, output_rows, output_columns)
    return (merged_query, merged_gate, merged_output, new_input, new_square, updated_gate_weight)


def solution(mesh):
    placed = (
        P("replica", "rollout"),
        P("replica", "rollout"),
        P("rollout", "replica"),
        P(None, None, "rollout", "replica"),
        P("replica", None, "rollout", None),
        P(None, None, "replica", "rollout"),
        P("replica", None, None, "rollout"),
        P(None, "replica", "rollout"),
        P("replica", None, "rollout"),
    )
    return jax.shard_map(
        on_device,
        mesh=mesh,
        in_specs=placed,
        out_specs=(
            P("replica", "rollout"),
            P("replica", "rollout"),
            P("rollout", "replica"),
            P(None, None, "rollout", "replica"),
            P(None, None, "replica", "rollout"),
            P(None, "replica", "rollout"),
        ),
        check_vma=False,
    )
```

profile of v0, /device:TPU:0, one launch (start us, length us, event | category | flops | bytes accessed | tf_op | source)
XLA Modules:
  0.0 170.0 jit_solution(4795390568116291196)
XLA Ops:
  9.4 29.0 %reduce-scatter.6.cloned.1.call-done = f32[1,2,16,1024]{3,2,1,0:T(8,128)} async-done(((f32[1,2,64,1024]{3,2,1,0:T(8,128)}), f32[1,2,16,1024]{3,2,1,0:T(8,128)}) %reduce-scatter.6.cloned.1.call-update) | async-done | bytes 131088 | tf_op jit(solution)/shard_map/reduce_scatter | solution.py:45
  38.3 1.2 fusion.35
  39.6 8.4 %all-gather = bf16[1,64,1024]{2,1,0:T(8,128)(2,1)S(1)} all-gather(bf16[1,16,1024]{2,1,0:T(8,128)(2,1)S(1)} %get-tuple-element.29), channel_id=2, replica_groups=mesh['replica'=4,'rollout'=8] {'replica'}, dimensions={1}, use_global_device_ids=true | all-gather | bytes 163840 | tf_op jit(solution)/shard_map/all_gather | solution.py:67
  47.9 14.2 %all-gather.2 = bf16[1,16,8192]{2,1,0:T(8,128)(2,1)S(1)} all-gather(bf16[1,16,1024]{2,1,0:T(8,128)(2,1)S(1)} %get-tuple-element.28), channel_id=4, replica_groups=mesh['replica'=4,'rollout'=8] {'rollout'}, dimensions={2}, use_global_device_ids=true | all-gather | bytes 294912 | tf_op jit(solution)/shard_map/all_gather | solution.py:63
  63.2 3.4 %all-to-all-start.1 = ((bf16[16,4,2048]{2,0,1:T(8,128)(2,1)}), bf16[16,4,2048]{2,0,1:T(8,128)(2,1)S(1)}, u32[]{:S(2)}, u32[]{:S(2)}) async-start(bf16[16,4,2048]{2,0,1:T(8,128)(2,1)} %copy.78), calls=%async_computation.4 | async-start | bytes 524288 | tf_op jit(solution)/shard_map/all_to_all | solution.py:71
  66.6 1.0 fusion.36
  67.6 1.2 fusion.29
  69.6 1.4 fusion.20
  71.0 1.4 bitcast_subtract_fusion
  72.4 14.7 %all_gather.15 = bf16[2,8192,16]{1,2,0:T(8,128)(2,1)S(1)} all-gather(bf16[2,1024,16]{1,2,0:T(8,128)(2,1)S(1)} %slice.62), channel_id=1, replica_groups=mesh['replica'=4,'rollout'=8] {'rollout'}, dimensions={1}, use_global_device_ids=true | all-gather | bytes 589824 | tf_op jit(solution)/shard_map/all_gather | solution.py:62
  87.1 6.6 %copy.72 = bf16[2,8192,16]{2,0,1:T(2,128)(2,1)} copy(bf16[2,8192,16]{1,2,0:T(8,128)(2,1)S(1)} %all_gather.15) | data formatting | bytes 1048576 | tf_op jit(solution)/shard_map/all_gather | solution.py:62
  93.7 6.5 %reshape.95 = bf16[4,2,32768]{2,1,0:T(2,128)(2,1)} reshape(bf16[8192,2,16]{2,1,0:T(2,128)(2,1)} %bitcast.157) | data formatting | bytes 1048576
  100.3 0.9 copy.83
  101.2 8.9 %all-gather.1 = bf16[1,1024,64]{1,2,0:T(8,128)(2,1)S(1)} all-gather(bf16[1,1024,16]{1,2,0:T(8,128)(2,1)S(1)} %slice.66), channel_id=3, replica_groups=mesh['replica'=4,'rollout'=8] {'replica'}, dimensions={2}, use_global_device_ids=true | all-gather | bytes 163840 | tf_op jit(solution)/shard_map/all_gather | solution.py:66
  110.1 3.5 %all-to-all-start = ((bf16[4,2,32768]{2,1,0:T(2,128)(2,1)}), bf16[4,2,32768]{2,1,0:T(2,128)(2,1)S(1)}, u32[]{:S(2)}, u32[]{:S(2)}) async-start(bf16[4,2,32768]{2,1,0:T(2,128)(2,1)} %reshape.95), calls=%async_computation.1 | async-start | bytes 1048576 | tf_op jit(solution)/shard_map/all_to_all | solution.py:70
  113.6 5.5 %add_convert_fusion.1 = bf16[1024,2048]{1,0:T(8,128)(2,1)} fusion(bf16[1024,2048]{1,0:T(8,128)(2,1)} %param.11, bf16[64,2048]{1,0:T(8,128)(2,1)S(1)} %bitcast.161, bf16[1,1024,64]{1,2,0:T(8,128)(2,1)S(1)} %all-gather.1), kind=kOutput, calls=%fused_computation.1 | convolution fusion | flops 276824064 | bytes 8781824 | tf_op jit(solution)/shard_map/dot_general | solution.py:28
  119.1 1.1 fusion.9
  120.2 10.9 %all_gather.17 = bf16[64,3584]{1,0:T(8,128)(2,1)S(1)} all-gather(bf16[16,3584]{1,0:T(8,128)(2,1)S(1)} %fusion.9), channel_id=1, replica_groups=mesh['replica'=4,'rollout'=8] {'replica'}, dimensions={0}, use_global_device_ids=true | all-gather | bytes 573440 | tf_op jit(solution)/shard_map/all_gather | solution.py:68
  131.0 1.1 divide_subtract_fusion
  132.1 0.9 pad_maximum_fusion
  133.0 4.1 %reshape.96 = bf16[8192,2,16]{2,1,0:T(2,128)(2,1)} reshape(bf16[4,2,32768]{2,1,0:T(2,128)(2,1)S(1)} %all-to-all-done) | data formatting | bytes 1048576
  137.1 9.7 %copy.84 = bf16[2,4,2048,16]{2,1,3,0:T(4,128)(2,1)S(1)} copy(bf16[2,4,2048,16]{3,0,2,1:T(2,128)(2,1)} %bitcast.158) | data formatting | bytes 1048576 | tf_op jit(solution)/shard_map/all_to_all | solution.py:70
  147.3 5.5 %add_convert_fusion.2 = bf16[2048,1024]{1,0:T(8,128)(2,1)} fusion(bf16[2048,1024]{1,0:T(8,128)(2,1)} %param.9, bf16[2048,64]{0,1:T(8,128)(2,1)S(1)} %bitcast.162, bf16[1,64,1024]{2,1,0:T(8,128)(2,1)S(1)} %all-gather), kind=kOutput, calls=%fused_computation.2 | convolution fusion | flops 276824064 | bytes 8781824 | tf_op jit(solution)/shard_map/dot_general | solution.py:28
  152.8 10.7 %add_convert_fusion = bf16[2048,3584]{1,0:T(8,128)(2,1)} fusion(bf16[2048,3584]{1,0:T(8,128)(2,1)} %param.10, bf16[2048,64]{0,1:T(8,128)(2,1)S(1)} %bitcast.160, bf16[64,3584]{1,0:T(8,128)(2,1)S(1)} %all_gather.17), kind=kOutput, calls=%fused_computation | convolution fusion | flops 968884224 | bytes 30081024 | tf_op jit(solution)/shard_map/dot_general | solution.py:28
  (22 shorter events, 4.6 us)
Async XLA Ops:
  7.2 31.2 %reduce-scatter.6.cloned.1.call-start = ((), (), s32[]{:S(2)}) async-start(), calls=%async_computation.6 | async-start | bytes 655360 | tf_op jit(solution)/shard_map/reduce_scatter | solution.py:45
  7.9 61.7 %reduce-scatter.4.cloned.1.call-start = ((), (), s32[]{:S(2)}) async-start(), calls=%async_computation.5 | async-start | bytes 983040 | tf_op jit(solution)/shard_map/reduce_scatter | solution.py:44
  8.6 110.4 %reduce-scatter.8.cloned.1.call-start = ((), (), s32[]{:S(2)}) async-start(), calls=%async_computation.7 | async-start | bytes 1146880 | tf_op jit(solution)/shard_map/reduce_scatter | solution.py:46
  63.2 46.9 %all-to-all-start.1 = ((bf16[16,4,2048]{2,0,1:T(8,128)(2,1)}), bf16[16,4,2048]{2,0,1:T(8,128)(2,1)S(1)}, u32[]{:S(2)}, u32[]{:S(2)}) async-start(bf16[16,4,2048]{2,0,1:T(8,128)(2,1)} %copy.78), calls=%async_computation.4 | async-start | bytes 524288 | tf_op jit(solution)/shard_map/all_to_all | solution.py:71
  93.7 25.3 %copy-start = (f32[3,16,3584]{2,1,0:T(8,128)S(1)}, f32[3,16,3584]{2,1,0:T(8,128)}, u32[]{:S(2)}) copy-start(f32[3,16,3584]{2,1,0:T(8,128)} %param.16) | copy-start | bytes 2064388
  110.1 22.9 %all-to-all-start = ((bf16[4,2,32768]{2,1,0:T(2,128)(2,1)}), bf16[4,2,32768]{2,1,0:T(2,128)(2,1)S(1)}, u32[]{:S(2)}, u32[]{:S(2)}) async-start(bf16[4,2,32768]{2,1,0:T(2,128)(2,1)} %reshape.95), calls=%async_computation.1 | async-start | bytes 1048576 | tf_op jit(solution)/shard_map/all_to_all | solution.py:70
Sparse Core Ops, SparseCore 0:
  10.8 27.4 reduce-scatter.5
  41.5 26.0 reduce-scatter.3
  70.8 26.8 reduce-scatter.7
where the time goes:
time: 171 us; the launch traced here: 170 us
  blocking collectives  57.1 us (33%)
  waiting for transfers between devices  31 us (18%)
  local copies, waits for them, and re-layouts  29.3 us (17%)
  matrix products  21.6 us (13%)
  between operations  13.8 us (8%)
  other arithmetic  10 us (6%)
  starting transfers between devices  7 us (4%)
    reduce_scatter x1, waiting for transfers between devices, on_device(): lax.psum_scatter(square_parts, 'replica', scatter_dimension=2, tiled=True)  29 us
    dot_general x3, matrix products, merge_weight(): weight_change = jnp.dot(left, right, preferred_element_type=jnp.float32)  21.6 us
    all_gather x1, blocking collectives, on_device(): lax.all_gather(input_factor[:2], 'rollout', axis=1, tiled=True)  14.7 us
    all_gather x1, blocking collectives, on_device(): lax.all_gather(square_factor[1], 'rollout', axis=1, tiled=True)  14.2 us
    unnamed x5, local copies, waits for them, and re-layouts  11.4 us
    all_gather x1, blocking collectives, on_device(): lax.all_gather(gate_factor, 'replica', axis=0, tiled=True)  10.9 us
    all_to_all x1, local copies, waits for them, and re-layouts, on_device(): lax.all_to_all(column_slab, 'replica', split_axis=1, concat_axis=2, tiled...  9.67 us
    all_gather x1, blocking collectives, on_device(): lax.all_gather(input_factor[2], 'replica', axis=1, tiled=True)  8.89 us
  transfers between devices with their start and end apart: 5, of which 1 were waited for; matrix products, arithmetic and copies ran while one was open for 18% of the time, Pallas kernels for 0%

commit v1 on v0

v1 whole, which is shorter than its diff:
```python
import functools

import jax
import jax.numpy as jnp
from jax import lax
from jax.experimental import pallas as pl
from jax.experimental.pallas import tpu as pltpu
from jax.sharding import PartitionSpec as P

STEP = 3

first_moment_decay = 0.9
beta_second = 0.999
learn_rate = 0.05
epsilon = 1e-08
adapter_scale = 2.0

MESH = pl.DeviceIdType.MESH
BF16 = jnp.bfloat16
F32 = jnp.float32


def adam_update(param, first, second, grad):
    first_new = first_moment_decay * first + (1.0 - first_moment_decay) * grad
    second_new = beta_second * second + (1.0 - beta_second) * grad * grad
    fix_first = 1.0 - first_moment_decay**STEP
    fix_second = 1.0 - beta_second**STEP
    param_new = param - learn_rate * (first_new / fix_first) / (
        jnp.sqrt(second_new / fix_second) + epsilon
    )
    return (param_new, first_new, second_new)


def exchange_kernel(
    n, lines, width,
    in_parts, sq_parts, ga_parts, in_state, sq_state, ga_state, w_query, w_gate, w_out,
    slab, pair, gate, in_new, sq_new, ga_new, v_query, v_gate, v_out,
    in_raw, sq_raw, ga_raw, in_old, sq_old, ga_old,
    send0, send1, send2, recv0, recv1, recv2, line,
    load_sem, state_sem, weight_sem, rs_send, rs_recv, line_send, line_recv,
    swap_send, swap_recv, core_send, core_recv, ag_send, ag_recv,
):
    me = lax.axis_index("replica")
    spot = lax.axis_index("rollout")
    place, core = spot // 2, lax.rem(spot, 2)
    mate = place * 2 + (1 - core)
    rows = in_old.shape[2]

    pieces = (
        (
            (in_parts.at[0, 0], in_raw.at[0], 0, in_old.at[0], in_new.at[0]),
            (in_parts.at[0, 1], in_raw.at[1], width, in_old.at[1], in_new.at[1]),
            (sq_parts.at[0, 1], sq_raw.at[1], 2 * width, sq_old.at[1], sq_new.at[1]),
        ),
        (
            (in_parts.at[0, 2], in_raw.at[2], 0, in_old.at[2], in_new.at[2]),
            (sq_parts.at[0, 0], sq_raw.at[0], width, sq_old.at[0], sq_new.at[0]),
        ),
        ((ga_parts.at[0], ga_raw, 0, ga_old, ga_new),),
    )
    sends, recvs = (send0, send1, send2), (recv0, recv1, recv2)

    loads = []
    for group in pieces:
        for source, raw, *_ in group:
            loads.append(pltpu.make_async_copy(source, raw, load_sem.at[len(loads)]))
    states = [
        pltpu.make_async_copy(source, old, state_sem.at[i])
        for i, (source, old) in enumerate(
            ((in_state, in_old), (sq_state, sq_old), (ga_state, ga_old))
        )
    ]
    weights = [
        pltpu.make_async_copy(source, held, weight_sem.at[i])
        for i, (source, held) in enumerate(
            ((w_gate, v_gate), (w_query, v_query), (w_out, v_out))
        )
    ]
    for copy in loads + states + weights:
        copy.start()

    barrier = pltpu.get_barrier_semaphore()
    for d in range(1, n):
        pl.semaphore_signal(
            barrier, inc=1, device_id=(lax.rem(me + d, n), spot), device_id_type=MESH
        )
    for d in range(1, lines):
        pl.semaphore_signal(
            barrier, inc=1, device_id=(me, lax.rem(place + d, lines) * 2 + core), device_id_type=MESH
        )
    pl.semaphore_signal(barrier, inc=1, device_id=(me, mate), device_id_type=MESH)

    def scatter(g, d):
        peer = lax.rem(me + d, n)
        return pltpu.make_async_remote_copy(
            src_ref=sends[g].at[peer], dst_ref=recvs[g].at[d - 1],
            send_sem=rs_send.at[g, d - 1], recv_sem=rs_recv.at[g, d - 1],
            device_id=(peer, spot), device_id_type=MESH,
        )

    def along(d):
        return pltpu.make_async_remote_copy(
            src_ref=line.at[place], dst_ref=line.at[place],
            send_sem=line_send.at[d - 1], recv_sem=line_recv.at[d - 1],
            device_id=(me, lax.rem(place + d, lines) * 2 + core), device_id_type=MESH,
        )

    def swap(d, peer):
        return pltpu.make_async_remote_copy(
            src_ref=line.at[peer], dst_ref=slab.at[core, me],
            send_sem=swap_send.at[d], recv_sem=swap_recv.at[me],
            device_id=(peer, spot), device_id_type=MESH,
        )

    def across(owner):
        return pltpu.make_async_remote_copy(
            src_ref=slab.at[core, owner], dst_ref=slab.at[core, owner],
            send_sem=core_send.at[owner], recv_sem=core_recv.at[owner],
            device_id=(me, mate), device_id_type=MESH,
        )

    def gather(g, d):
        full = (pair, gate)[g]
        return pltpu.make_async_remote_copy(
            src_ref=full.at[me], dst_ref=full.at[me],
            send_sem=ag_send.at[g, d - 1], recv_sem=ag_recv.at[g, d - 1],
            device_id=(lax.rem(me + d, n), spot), device_id_type=MESH,
        )

    at_load = 0
    for g, group in enumerate(pieces):
        for _, raw, start, *_ in group:
            loads[at_load].wait()
            at_load += 1
            span = raw.shape[1]
            for j in range(n):
                sends[g][j, :, start : start + span] = raw[j * rows : (j + 1) * rows, :].astype(BF16)
        if g == 0:
            pl.semaphore_wait(barrier, n - 1 + lines - 1 + 1)
        for d in range(1, n):
            scatter(g, d).start()
    for copy in states:
        copy.wait()

    def update(g, factor):
        for d in range(1, n):
            scatter(g, d).wait_recv()
        mine = pl.ds(pl.multiple_of(me * rows, rows), rows)
        for _, raw, start, old, new in pieces[g]:
            span = raw.shape[1]
            step = 512 if span % 512 == 0 else 256
            for c in range(0, span, step):
                here, there = slice(c, c + step), slice(start + c, start + c + step)
                grad = raw[mine, here]
                for d in range(1, n):
                    grad = grad + recvs[g][d - 1, :, there].astype(F32)
                param, first, second = adam_update(old[0, :, here], old[1, :, here], old[2, :, here], grad)
                new[0, :, here] = param
                new[1, :, here] = first
                new[2, :, here] = second
                factor[:, there] = param.astype(BF16)

    def pass_on(d):
        if d:
            along_from = lax.rem(place + lines - d, lines)
            pltpu.make_async_remote_copy(
                src_ref=line.at[along_from], dst_ref=line.at[along_from],
                send_sem=line_send.at[d - 1], recv_sem=line_recv.at[d - 1],
                device_id=(me, lax.rem(place + d, lines) * 2 + core), device_id_type=MESH,
            ).wait_recv()
        peer = lax.rem(place + lines - d, lines)

        @pl.when(peer != me)
        def _():
            swap(d, peer).start()

        @pl.when(peer == me)
        def _():
            slab[core, me] = line[me]

    update(0, line.at[place])
    for d in range(1, lines):
        along(d).start()
    pass_on(0)
    update(1, pair.at[me])
    for d in range(1, n):
        gather(0, d).start()
    pass_on(1)
    update(2, gate.at[me])
    for d in range(1, n):
        gather(1, d).start()
    for d in range(2, lines):
        pass_on(d)

    across(me).start()
    for d in range(1, n):
        owner = lax.rem(me + d, n)
        pltpu.make_async_remote_copy(
            src_ref=line.at[me], dst_ref=slab.at[core, owner],
            send_sem=swap_send.at[d], recv_sem=swap_recv.at[owner],
            device_id=(owner, spot), device_id_type=MESH,
        ).wait_recv()
        across(owner).start()

    for copy in weights:
        copy.wait()
    for g in range(3):
        for d in range(1, n):
            scatter(g, d).wait_send()
    for d in range(1, lines):
        along(d).wait_send()
    for d in range(lines):
        peer = lax.rem(place + lines - d, lines)

        @pl.when(peer != me)
        def _():
            swap(d, peer).wait_send()

    for g, full in enumerate((pair, gate)):
        for d in range(1, n):
            gather(g, d).wait_send()
            owner = lax.rem(me + n - d, n)
            pltpu.make_async_remote_copy(
                src_ref=full.at[owner], dst_ref=full.at[owner],
                send_sem=ag_send.at[g, d - 1], recv_sem=ag_recv.at[g, d - 1],
                device_id=(lax.rem(me + d, n), spot), device_id_type=MESH,
            ).wait_recv()
    for d in range(n):
        owner = lax.rem(me + d, n)
        across(owner).wait_send()
        pltpu.make_async_remote_copy(
            src_ref=slab.at[1 - core, owner], dst_ref=slab.at[1 - core, owner],
            send_sem=core_send.at[owner], recv_sem=core_recv.at[owner],
            device_id=(me, mate), device_id_type=MESH,
        ).wait_recv()


def merge_kernel(
    width,
    slab, pair, gate, in_new, sq_new, ga_new, v_query, v_gate, v_out,
    m_query, m_gate, m_out, in_out, sq_out, ga_out,
    s_query, s_gate, s_out, state_sem, sem,
):
    n, rows = slab.shape[1], slab.shape[2]
    rank = n * rows

    states = [
        pltpu.make_async_copy(new, out, state_sem.at[i])
        for i, (new, out) in enumerate(((in_new, in_out), (sq_new, sq_out), (ga_new, ga_out)))
    ]
    for copy in states:
        copy.start()

    def flat(block):
        if rows % 16 == 0:
            return block.reshape(rank, block.shape[-1])
        return block.astype(F32).reshape(rank, block.shape[-1]).astype(BF16)

    def merge(which, held, staged, merged, left, rights, first, count):
        slots, tile = staged.shape[:2]
        done = first // tile

        def out_copy(i):
            slot = lax.rem(i, slots)
            at = pl.ds(pl.multiple_of(i * tile, tile), tile)
            return pltpu.make_async_copy(staged.at[slot], merged.at[at], sem.at[which, slot])

        def body(i, _):
            whole = done + i
            slot = lax.rem(whole, slots)

            @pl.when(whole >= slots)
            def _():
                out_copy(whole - slots).wait()

            at = pl.ds(pl.multiple_of(whole * tile, tile), tile)
            lhs = left(pl.ds(pl.multiple_of(i * tile, tile), tile)) * adapter_scale
            for start, span, right in rights:
                step = 512 if span % 512 == 0 else 256
                for c in range(0, span, step):
                    change = lax.dot_general(
                        lhs, right(slice(c, c + step)), (((0,), (0,)), ((), ())),
                        preferred_element_type=F32,
                    )
                    there = slice(start + c, start + c + step)
                    staged[slot, :, there] = (held[at, there].astype(F32) + change).astype(BF16)
            out_copy(whole).start()
            return 0

        lax.fori_loop(0, count // tile, body, 0)

    def drain(which, staged, merged):
        slots, tile = staged.shape[:2]
        steps = merged.shape[0] // tile
        for i in range(max(0, steps - slots), steps):
            pltpu.make_async_copy(
                staged.at[i % slots], merged.at[i * tile : (i + 1) * tile], sem.at[which, i % slots]
            ).wait()

    def slab_left(j, start):
        return lambda at: flat(slab[j, :, :, pl.ds(start + at.start, at.size)])

    hidden = gate.shape[2]
    for j in range(2):
        merge(
            0, v_gate, s_gate, m_gate, slab_left(j, width),
            ((0, hidden, lambda at: flat(gate[:, :, at])),), j * width, width,
        )
    for j in range(2):
        merge(
            1, v_query, s_query, m_query, slab_left(j, 0),
            ((0, width, lambda at: flat(pair[:, :, width + at.start : width + at.stop])),),
            j * width, width,
        )

    def out_right(j):
        return lambda at: flat(slab[j, :, :, 2 * width + at.start : 2 * width + at.stop])

    merge(
        2, v_out, s_out, m_out, lambda at: flat(pair[:, :, at]),
        ((0, width, out_right(0)), (width, width, out_right(1))), 0, width,
    )
    for which, (staged, merged) in enumerate(((s_gate, m_gate), (s_query, m_query), (s_out, m_out))):
        drain(which, staged, merged)
    for copy in states:
        copy.wait()


def on_device(
    n, lines,
    w_query, gate_weight, w_output, input_state, input_parts,
    square_state, square_parts, gate_state, gate_parts,
):
    in_state, in_parts = jnp.swapaxes(input_state, 2, 3), jnp.swapaxes(input_parts, 2, 3)
    rank, width = in_parts.shape[2:]
    rows = in_state.shape[2]
    hidden = gate_parts.shape[2]
    spans = (3 * width, 2 * width, hidden)
    dma = pltpu.SemaphoreType.DMA
    hbm = pl.BlockSpec(memory_space=pltpu.HBM)
    vmem = pl.BlockSpec(memory_space=pltpu.VMEM)

    held = pl.pallas_call(
        functools.partial(exchange_kernel, n, lines, width),
        out_shape=[
            pltpu.VMEM((2, n, rows, 3 * width), BF16),
            pltpu.VMEM((n, rows, 2 * width), BF16),
            pltpu.VMEM((n, rows, hidden), BF16),
            pltpu.VMEM(in_state.shape, F32),
            pltpu.VMEM(square_state.shape, F32),
            pltpu.VMEM(gate_state.shape, F32),
            pltpu.VMEM(w_query.shape, BF16),
            pltpu.VMEM(gate_weight.shape, BF16),
            pltpu.VMEM(w_output.shape, BF16),
        ],
        in_specs=[hbm] * 9,
        out_specs=[vmem] * 9,
        scratch_shapes=[
            pltpu.VMEM(in_parts.shape[1:], F32),
            pltpu.VMEM(square_parts.shape[1:], F32),
            pltpu.VMEM(gate_parts.shape[1:], F32),
            pltpu.VMEM(in_state.shape, F32),
            pltpu.VMEM(square_state.shape, F32),
            pltpu.VMEM(gate_state.shape, F32),
            *(pltpu.VMEM((n, rows, span), BF16) for span in spans),
            *(pltpu.VMEM((n - 1, rows, span), BF16) for span in spans),
            pltpu.VMEM((lines, rows, 3 * width), BF16),
            dma((6,)), dma((3,)), dma((3,)),
            dma((3, n - 1)), dma((3, n - 1)),
            dma((lines - 1,)), dma((lines - 1,)),
            dma((lines,)), dma((n,)),
            dma((n,)), dma((n,)),
            dma((2, n - 1)), dma((2, n - 1)),
        ],
        compiler_params=pltpu.CompilerParams(
            collective_id=0, has_side_effects=True, vmem_limit_bytes=16 * 2**20
        ),
        name="exchange",
    )(
        *(
            pltpu.with_memory_space_constraint(x, pltpu.HBM)
            for x in (
                in_parts, square_parts, gate_parts, in_state, square_state, gate_state,
                w_query, gate_weight, w_output,
            )
        )
    )
    merged_query, merged_gate, merged_output, new_input, new_square, new_gate = pl.pallas_call(
        functools.partial(merge_kernel, width),
        out_shape=[
            jax.ShapeDtypeStruct(w_query.shape, BF16),
            jax.ShapeDtypeStruct(gate_weight.shape, BF16),
            jax.ShapeDtypeStruct(w_output.shape, BF16),
            jax.ShapeDtypeStruct(in_state.shape, F32),
            jax.ShapeDtypeStruct(square_state.shape, F32),
            jax.ShapeDtypeStruct(gate_state.shape, F32),
        ],
        in_specs=[vmem] * 9,
        out_specs=[hbm] * 6,
        scratch_shapes=[
            *(pltpu.VMEM((4, 128, w.shape[1]), BF16) for w in (w_query, gate_weight, w_output)),
            dma((3,)),
            dma((3, 4)),
        ],
        compiler_params=pltpu.CompilerParams(vmem_limit_bytes=16 * 2**20),
        name="merge",
    )(*(pltpu.with_memory_space_constraint(x, pltpu.VMEM) for x in held))
    return (merged_query, merged_gate, merged_output, jnp.swapaxes(new_input, 2, 3), new_square, new_gate)


def solution(mesh):
    n, lines = mesh.shape["replica"], mesh.shape["rollout"] // 2
    assert n == lines
    return jax.shard_map(
        functools.partial(on_device, n, lines),
        mesh=mesh,
        in_specs=(
            P("replica", "rollout"),
            P("replica", "rollout"),
            P("rollout", "replica"),
            P(None, None, "rollout", "replica"),
            P("replica", None, "rollout", None),
            P(None, None, "replica", "rollout"),
            P("replica", None, None, "rollout"),
            P(None, "replica", "rollout"),
            P("replica", None, "rollout"),
        ),
        out_specs=(
            P("replica", "rollout"),
            P("replica", "rollout"),
            P("rollout", "replica"),
            P(None, None, "rollout", "replica"),
            P(None, None, "replica", "rollout"),
            P(None, "replica", "rollout"),
        ),
        check_vma=False,
    )
```

time: 171 us -> 47.2 us (0.28)
  blocking collectives: 57.1 us -> 0 us
  Pallas kernels: 0 us -> 46.1 us
  waiting for transfers between devices: 31 us -> 0 us
  local copies, waits for them, and re-layouts: 29.3 us -> 0 us
  matrix products: 21.6 us -> 0 us
  between operations: 13.8 us -> 0.64 us
  other arithmetic: 10 us -> 0 us
  starting transfers between devices: 7 us -> 0 us
    all_gather x5 -> x0, blocking collectives: 57.1 us -> none  [the longest x1 14.7 us: on_device(): lax.all_gather(input_factor[:2], 'rollout', axis=1, tiled=True)]
    pallas_call x0 -> x2, Pallas kernels: none -> 46.1 us  [the longest x1 31.5 us: on_device(): pl.pallas_call(functools.partial(exchange_kernel, n, lines, width), out_s...]
    reduce_scatter x3 -> x0, waiting for transfers between devices: 29 us -> none  [the longest x1 29 us: on_device(): lax.psum_scatter(square_parts, 'replica', scatter_dimension=2, tiled=True)]
    dot_general x3 -> x0, matrix products: 21.6 us -> none  [merge_weight(): weight_change = jnp.dot(left, right, preferred_element_type=jnp.float32)]
    unnamed x5 -> x0, local copies, waits for them, and re-layouts: 11.4 us -> none
    all_to_all x3 -> x0, local copies, waits for them, and re-layouts: 10.7 us -> none  [the longest x1 9.67 us: on_device(): lax.all_to_all(column_slab, 'replica', split_axis=1, concat_axis=2, tiled...]
    all_to_all x2 -> x0, starting transfers between devices: 6.89 us -> none  [the longest x1 3.48 us: on_device(): lax.all_to_all(column_slab, 'replica', split_axis=1, concat_axis=2, tiled...]
    all_gather x1 -> x0, local copies, waits for them, and re-layouts: 6.65 us -> none  [on_device(): lax.all_gather(input_factor[:2], 'rollout', axis=1, tiled=True)]
  transfers between devices with their start and end apart: 5 -> 0, of which waited for: 1 -> 0; matrix products, arithmetic and copies ran while one was open for 18% -> 0% of each run, Pallas kernels for 0% -> 0%
where the time goes in v1:
time: 47.2 us; the launch traced here: 46.8 us
  Pallas kernels  46.1 us (98%)
  between operations  0.64 us (1%)
    pallas_call x1, Pallas kernels, on_device(): pl.pallas_call(functools.partial(exchange_kernel, n, lines, width), out_s...  31.5 us
    pallas_call x1, Pallas kernels, on_device(): pl.pallas_call(functools.partial(merge_kernel, width), out_shape=[jax.Sha...  14.6 us

profile of v1, /device:TPU:0, one launch (start us, length us, event | category | flops | bytes accessed | tf_op | source)
XLA Modules:
  0.0 46.8 jit_solution(9182224038725083683)
XLA Ops:
  0.6 31.5 %exchange.1 = (bf16[2,4,16,3072]{3,2,1,0:T(8,128)(2,1)S(1)}, bf16[4,16,2048]{2,1,0:T(8,128)(2,1)S(1)}, bf16[4,16,3584]{2,1,0:T(8,128)(2,1)S(1)}, f32[3,3,16,1024...) custom-call(f32[1,3,64,1024]{3,2,1,0:T(8,128)} %bitcast.3, ...), custom_call_target="tpu_custom_call" | custom-call | tf_op jit(solution)/shard_map/exchange/pallas_call | solution.py:343
  32.2 14.6 %merge.1 = (bf16[2048,1024]{1,0:T(8,128)(2,1)}, bf16[2048,3584]{1,0:T(8,128)(2,1)}, bf16[1024,2048]{1,0:T(8,128)(2,1)}, f32[3,3,16,1024]{3,2,1,0:T(8,128)}, f32[...) custom-call(bf16[2,4,16,3072]{3,2,1,0:T(8,128)(2,1)S(1)} %get-tuple-element.21.slab, ...), custom_call_target="tpu_custom_call" | custom-call | tf_op jit(solution)/shard_map/merge/pallas_call | solution.py:388

commit v2 on v1

--- a/solution.py
+++ b/solution.py
@@ -274,14 +274,11 @@
                 out_copy(whole - slots).wait()
 
             at = pl.ds(pl.multiple_of(whole * tile, tile), tile)
-            lhs = left(pl.ds(pl.multiple_of(i * tile, tile), tile)) * adapter_scale
+            lhs = jnp.transpose(left(pl.ds(pl.multiple_of(i * tile, tile), tile)) * adapter_scale)
             for start, span, right in rights:
-                step = 512 if span % 512 == 0 else 256
+                step = 256
                 for c in range(0, span, step):
-                    change = lax.dot_general(
-                        lhs, right(slice(c, c + step)), (((0,), (0,)), ((), ())),
-                        preferred_element_type=F32,
-                    )
+                    change = jnp.dot(lhs, right(slice(c, c + step)), preferred_element_type=F32)
                     there = slice(start + c, start + c + step)
                     staged[slot, :, there] = (held[at, there].astype(F32) + change).astype(BF16)
             out_copy(whole).start()
@@ -398,9 +395,9 @@
         in_specs=[vmem] * 9,
         out_specs=[hbm] * 6,
         scratch_shapes=[
-            *(pltpu.VMEM((4, 128, w.shape[1]), BF16) for w in (w_query, gate_weight, w_output)),
+            *(pltpu.VMEM((3, 256, w.shape[1]), BF16) for w in (w_query, gate_weight, w_output)),
             dma((3,)),
-            dma((3, 4)),
+            dma((3, 3)),
         ],
         compiler_params=pltpu.CompilerParams(vmem_limit_bytes=16 * 2**20),
         name="merge",

time: 47.2 us -> 44.1 us (0.934)
  Pallas kernels: 46.1 us -> 43 us
    pallas_call x1, Pallas kernels: 14.6 us -> 11.5 us  [on_device(): pl.pallas_call(functools.partial(merge_kernel, width), out_shape=[jax.Sha...]
where the time goes in v2:
time: 44.1 us; the launch traced here: 43.6 us
  Pallas kernels  43 us (98%)
  between operations  0.64 us (1%)
    pallas_call x1, Pallas kernels, on_device(): pl.pallas_call(functools.partial(exchange_kernel, n, lines, width), out_s...  31.5 us
    pallas_call x1, Pallas kernels, on_device(): pl.pallas_call(functools.partial(merge_kernel, width), out_shape=[jax.Sha...  11.5 us

profile of v2, /device:TPU:0, one launch (start us, length us, event | category | flops | bytes accessed | tf_op | source)
XLA Modules:
  0.0 43.6 jit_solution(15317295088066039478)
XLA Ops:
  0.6 31.5 %exchange.1 = (bf16[2,4,16,3072]{3,2,1,0:T(8,128)(2,1)S(1)}, bf16[4,16,2048]{2,1,0:T(8,128)(2,1)S(1)}, bf16[4,16,3584]{2,1,0:T(8,128)(2,1)S(1)}, f32[3,3,16,1024...) custom-call(f32[1,3,64,1024]{3,2,1,0:T(8,128)} %bitcast.3, ...), custom_call_target="tpu_custom_call" | custom-call | tf_op jit(solution)/shard_map/exchange/pallas_call | solution.py:340
  32.2 11.5 %merge.1 = (bf16[2048,1024]{1,0:T(8,128)(2,1)}, bf16[2048,3584]{1,0:T(8,128)(2,1)}, bf16[1024,2048]{1,0:T(8,128)(2,1)}, f32[3,3,16,1024]{3,2,1,0:T(8,128)}, f32[...) custom-call(bf16[2,4,16,3072]{3,2,1,0:T(8,128)(2,1)S(1)} %get-tuple-element.21.slab, ...), custom_call_target="tpu_custom_call" | custom-call | tf_op jit(solution)/shard_map/merge/pallas_call | solution.py:385
